TPU v7x, 32 devices: a whole 2x2x4 slice. The times are simulated.
32 devices in a mesh: seq: 16 (over z, y, core), stream: 2 (over x).
Axes of the slice: x: 2, y: 2, z: 4, core: 2. Of those that a mesh axis runs over, the one named last changes fastest.
Arguments:
- tokens: bfloat16 [2, 8192, 768], P('stream', 'seq'), may hold values from -6 to 6
- lengths: int32 [16, 4], P('seq'), may hold values from 0 to 512, as said below
- cotangent: bfloat16 [2, 8192, 768], P('stream', 'seq'), may hold values from -6 to 6
- attn_gain: bfloat16 [768], P(('seq', 'stream')), may hold values from 0.099609375 to 1.8984375
- qkv_weight: bfloat16 [768, 2304], P(('seq', 'stream')), may hold values from -0.21875 to 0.21875
- out_weight: bfloat16 [768, 768], P(('seq', 'stream')), may hold values from -0.875 to 0.875
- mlp_gain: bfloat16 [768], P(('seq', 'stream')), may hold values from 0.099609375 to 1.8984375
- up_weight: bfloat16 [768, 3072], P(('seq', 'stream')), may hold values from -0.21875 to 0.21875
- up_bias: bfloat16 [3072], P(('seq', 'stream')), may hold values from -3 to 3
- down_weight: bfloat16 [3072, 768], P(('seq', 'stream')), may hold values from -0.109375 to 0.109375
- down_bias: bfloat16 [768], P(('seq', 'stream')), may hold values from -2 to 2
Outputs:
- layer_out: bfloat16 [2, 8192, 768], P('stream', 'seq')
- grad_tokens: float32 [2, 8192, 768], P('stream', 'seq')
- grad_attn_gain: float32 [768], P(('seq', 'stream'))
- grad_qkv_weight: float32 [768, 2304], P(('seq', 'stream'))
- grad_out_weight: float32 [768, 768], P(('seq', 'stream'))
- grad_mlp_gain: float32 [768], P(('seq', 'stream'))
- grad_up_weight: float32 [768, 3072], P(('seq', 'stream'))
- grad_up_bias: float32 [3072], P(('seq', 'stream'))
- grad_down_weight: float32 [3072, 768], P(('seq', 'stream'))
- grad_down_bias: float32 [768], P(('seq', 'stream'))
Inputs may be any that keep to these rules, and one draw needn't show every extreme that they name: `lengths`: each row sums to 512; a 0 is an empty slot; some row holds a single sequence of 512 tokens.
All inputs are finite; a program needn't handle non-finite values.
Results may differ from a plain program's by a relative error of at most 0.014.
Values may be sent and summed in bfloat16 or wider, within the bound.
No kernel may reach another device: no remote copies, remote signals or barrier semaphores. Data moves between devices by JAX's collectives and lax.ppermute only.
A program may use at most 192 MiB of HBM per device.

v0:
```python
from functools import partial
import math

import jax
import jax.numpy as jnp
from jax import lax
from jax.sharding import PartitionSpec as P

HEADS = 12
HEAD_DIM = 64
BLOCK = 16


EPSILON = 1e-05
NEG_FILL = -1e30


def shifted(block, axis, distance):
    devices = range(lax.axis_size(axis))
    route = [(i - distance, i) for i in devices if i - distance in devices]
    return lax.ppermute(block, axis, route)


def doc_layout(pack_lengths, row_count):
    seq_ends = jnp.cumsum(pack_lengths)
    row_index = jnp.arange(row_count, dtype=jnp.int32)
    passed = seq_ends[None, :] <= row_index[:, None]
    doc_ids = jnp.sum(passed.astype(jnp.int32), axis=1)
    starts = jnp.max(jnp.where(passed, seq_ends[None, :], 0), axis=1)
    return (doc_ids, row_index - starts)


def rotary_tables(positions, head_size):
    half_size = head_size // 2
    frequency = jnp.exp(
        jnp.arange(half_size, dtype=jnp.float32) * (-2.0 * math.log(10000.0) / head_size)
    )
    angles = positions.astype(jnp.float32)[:, None] * frequency[None, :]
    return (jnp.cos(angles), jnp.sin(angles))


def rotate(tensor, cosine, sine_part):
    half_size = tensor.shape[-1] // 2
    first_half = tensor[..., :half_size]
    second_half = tensor[..., half_size:]
    cos_heads = cosine[:, None, :]
    sin_heads = sine_part[:, None, :]
    return jnp.concatenate(
        [
            first_half * cos_heads - second_half * sin_heads,
            second_half * cos_heads + first_half * sin_heads,
        ],
        axis=-1,
    )


def rotate_back(tensor, cosine, sine_part):
    half_size = tensor.shape[-1] // 2
    first_half = tensor[..., :half_size]
    second_half = tensor[..., half_size:]
    cos_heads = cosine[:, None, :]
    sin_heads = sine_part[:, None, :]
    return jnp.concatenate(
        [
            first_half * cos_heads + second_half * sin_heads,
            second_half * cos_heads - first_half * sin_heads,
        ],
        axis=-1,
    )


def norm_rows(values, gain_row):
    center = values - jnp.mean(values, axis=-1, keepdims=True)
    inverse_dev = lax.rsqrt(jnp.mean(center * center, axis=-1, keepdims=True) + EPSILON)
    normed = center * inverse_dev
    return (normed * gain_row, normed, inverse_dev)


def norm_back(grad_out, normed, inverse_dev, gain_row):
    grad_norm = grad_out * gain_row
    grad_gain = jnp.sum(grad_out * normed, axis=0)
    grad_in = inverse_dev * (
        grad_norm
        - jnp.mean(grad_norm, axis=-1, keepdims=True)
        - normed * jnp.mean(grad_norm * normed, axis=-1, keepdims=True)
    )
    return (grad_in, grad_gain)


def local(
    tokens,
    lengths,
    cotangent,
    attn_gain,
    qkv_weight,
    out_weight,
    mlp_gain,
    up_weight,
    up_bias,
    down_weight,
    down_bias,
):
    row_count = tokens.shape[1]
    model_width = tokens.shape[2]
    head_scale = HEAD_DIM ** (-0.5)
    block_rows = min(512, row_count)
    block_count = row_count // block_rows
    attn_set = (
        lax.all_gather(attn_gain, ("seq", "stream"), axis=0, tiled=True),
        lax.all_gather(qkv_weight, ("seq", "stream"), axis=0, tiled=True),
        lax.all_gather(out_weight, ("seq", "stream"), axis=0, tiled=True),
    )
    gain_one, qkv_full, out_full = attn_set
    resid_in = tokens[0].astype(jnp.float32)
    first_full, normed_one, inverse_one = norm_rows(resid_in, gain_one.astype(jnp.float32))
    first_in = first_full.astype(jnp.bfloat16)
    projected = jnp.dot(first_in, qkv_full, preferred_element_type=jnp.float32)
    doc_ids, positions = doc_layout(lengths[0], row_count)
    cosine, sine_part = rotary_tables(positions, HEAD_DIM)
    queries = rotate(
        projected[:, :model_width].reshape(row_count, HEADS, HEAD_DIM), cosine, sine_part
    ).astype(jnp.bfloat16)
    own_keys = rotate(
        projected[:, model_width : 2 * model_width].reshape(row_count, HEADS, HEAD_DIM),
        cosine,
        sine_part,
    ).astype(jnp.bfloat16)
    own_values = projected[:, 2 * model_width :].astype(jnp.bfloat16)
    partner = shifted(
        jnp.stack([own_keys.reshape(row_count, model_width), own_values]), "stream", 1
    )
    key_rows = jnp.concatenate([own_keys, partner[0].reshape(row_count, HEADS, HEAD_DIM)], axis=0)
    value_rows = jnp.concatenate([own_values, partner[1]], axis=0).reshape(
        2 * row_count, HEADS, HEAD_DIM
    )
    is_noisy = lax.axis_index("stream") == 1
    block_ids = positions // BLOCK
    same_doc = doc_ids[:, None] == doc_ids[None, :]
    own_ok = same_doc & jnp.where(
        is_noisy, block_ids[:, None] == block_ids[None, :], block_ids[:, None] >= block_ids[None, :]
    )
    partner_ok = same_doc & (block_ids[:, None] > block_ids[None, :]) & is_noisy
    allowed = jnp.concatenate([own_ok, partner_ok], axis=1).reshape(
        block_count, block_rows, 2 * row_count
    )
    query_blocks = queries.reshape(block_count, block_rows, HEADS, HEAD_DIM)

    def scores_of(query_block, mask_block, key_set):
        raw_scores = jnp.einsum(
            "qhd,khd->hqk", query_block, key_set, preferred_element_type=jnp.float32
        )
        return jnp.where(mask_block[None], raw_scores * head_scale, NEG_FILL)

    def run_forward(key_set, value_set, mask_set):

        def attend(running, block_in):
            query_block, mask_block = block_in
            scores = scores_of(query_block, mask_block, key_set)
            row_max = jnp.max(scores, axis=-1, keepdims=True)
            exponent = jnp.exp(scores - row_max)
            row_sum = jnp.sum(exponent, axis=-1, keepdims=True)
            weights_low = (exponent / row_sum).astype(jnp.bfloat16)
            mixed_rows = jnp.einsum(
                "hqk,khd->qhd", weights_low, value_set, preferred_element_type=jnp.float32
            )
            return (running, (mixed_rows, (row_max + jnp.log(row_sum))[..., 0]))

        return lax.scan(attend, 0, (query_blocks, mask_set))[1]

    attn_rows, log_sums = lax.cond(
        is_noisy,
        lambda: run_forward(key_rows, value_rows, allowed),
        lambda: run_forward(key_rows[:row_count], value_rows[:row_count], allowed[..., :row_count]),
    )
    attn_low = attn_rows.reshape(row_count, model_width).astype(jnp.bfloat16)
    after_attn = resid_in + jnp.dot(attn_low, out_full, preferred_element_type=jnp.float32)
    mlp_set = (
        lax.all_gather(mlp_gain, ("seq", "stream"), axis=0, tiled=True),
        lax.all_gather(up_weight, ("seq", "stream"), axis=0, tiled=True),
        lax.all_gather(up_bias, ("seq", "stream"), axis=0, tiled=True),
        lax.all_gather(down_weight, ("seq", "stream"), axis=0, tiled=True),
        lax.all_gather(down_bias, ("seq", "stream"), axis=0, tiled=True),
    )
    gain_two, up_full, up_bias_full, down_full, down_bias_full = mlp_set
    second_full, normed_two, inverse_two = norm_rows(after_attn, gain_two.astype(jnp.float32))
    second_in = second_full.astype(jnp.bfloat16)
    pre_act = jnp.dot(second_in, up_full, preferred_element_type=jnp.float32) + up_bias_full.astype(
        jnp.float32
    )
    activated = jax.nn.gelu(pre_act, approximate=True).astype(jnp.bfloat16)
    layer_full = (
        after_attn
        + jnp.dot(activated, down_full, preferred_element_type=jnp.float32)
        + down_bias_full.astype(jnp.float32)
    )
    layer_out = layer_full.astype(jnp.bfloat16)[None]
    mlp_back = (
        lax.all_gather(mlp_gain, ("seq", "stream"), axis=0, tiled=True),
        lax.all_gather(up_weight, ("seq", "stream"), axis=0, tiled=True),
        lax.all_gather(up_bias, ("seq", "stream"), axis=0, tiled=True),
        lax.all_gather(down_weight, ("seq", "stream"), axis=0, tiled=True),
        lax.all_gather(down_bias, ("seq", "stream"), axis=0, tiled=True),
    )
    gain_back_two, up_back, _, down_back, _ = mlp_back
    grad_top = cotangent[0]
    grad_down_bias = jnp.sum(grad_top, axis=0, dtype=jnp.float32)
    grad_down_w = jnp.einsum("tf,td->fd", activated, grad_top, preferred_element_type=jnp.float32)
    grad_act = jnp.einsum("td,fd->tf", grad_top, down_back, preferred_element_type=jnp.float32)
    _, gelu_pull = jax.vjp(partial(jax.nn.gelu, approximate=True), pre_act)
    grad_pre = gelu_pull(grad_act)[0].astype(jnp.bfloat16)
    grad_up_b = jnp.sum(grad_pre, axis=0, dtype=jnp.float32)
    grad_up_w = jnp.einsum("td,tf->df", second_in, grad_pre, preferred_element_type=jnp.float32)
    grad_second = jnp.einsum("tf,df->td", grad_pre, up_back, preferred_element_type=jnp.float32)
    grad_mid, grad_gain_two = norm_back(
        grad_second, normed_two, inverse_two, gain_back_two.astype(jnp.float32)
    )
    grad_after = grad_top.astype(jnp.float32) + grad_mid
    mlp_owned = (
        lax.psum_scatter(grad_gain_two, ("seq", "stream"), scatter_dimension=0, tiled=True),
        lax.psum_scatter(grad_up_w, ("seq", "stream"), scatter_dimension=0, tiled=True),
        lax.psum_scatter(grad_up_b, ("seq", "stream"), scatter_dimension=0, tiled=True),
        lax.psum_scatter(grad_down_w, ("seq", "stream"), scatter_dimension=0, tiled=True),
        lax.psum_scatter(grad_down_bias, ("seq", "stream"), scatter_dimension=0, tiled=True),
    )
    attn_back = (
        lax.all_gather(attn_gain, ("seq", "stream"), axis=0, tiled=True),
        lax.all_gather(qkv_weight, ("seq", "stream"), axis=0, tiled=True),
        lax.all_gather(out_weight, ("seq", "stream"), axis=0, tiled=True),
    )
    gain_back_one, qkv_back, out_back = attn_back
    grad_attn_low = grad_after.astype(jnp.bfloat16)
    grad_out_w = jnp.einsum(
        "td,te->de", attn_low, grad_attn_low, preferred_element_type=jnp.float32
    )
    grad_mixed = jnp.einsum(
        "te,de->td", grad_attn_low, out_back, preferred_element_type=jnp.float32
    ).astype(jnp.bfloat16)
    grad_mixed = grad_mixed.reshape(block_count, block_rows, HEADS, HEAD_DIM)

    def run_backward(key_set, value_set, mask_set):

        def attend_back(running, block_in):
            key_acc, value_acc = running
            query_block, mask_block, lse_block, grad_block = block_in
            scores = scores_of(query_block, mask_block, key_set)
            probs_full = jnp.exp(scores - lse_block[..., None])
            grad_probs = jnp.einsum(
                "qhd,khd->hqk", grad_block, value_set, preferred_element_type=jnp.float32
            )
            delta_rows = jnp.sum(grad_probs * probs_full, axis=-1, keepdims=True)
            grad_scores = (probs_full * (grad_probs - delta_rows) * head_scale).astype(jnp.bfloat16)
            grad_query = jnp.einsum(
                "hqk,khd->qhd", grad_scores, key_set, preferred_element_type=jnp.float32
            )
            key_acc = key_acc + jnp.einsum(
                "hqk,qhd->khd", grad_scores, query_block, preferred_element_type=jnp.float32
            )
            value_acc = value_acc + jnp.einsum(
                "hqk,qhd->khd",
                probs_full.astype(jnp.bfloat16),
                grad_block,
                preferred_element_type=jnp.float32,
            )
            return ((key_acc, value_acc), grad_query)

        zero_state = jnp.zeros(key_set.shape, jnp.float32)
        return lax.scan(
            attend_back, (zero_state, zero_state), (query_blocks, mask_set, log_sums, grad_mixed)
        )

    def backward_own():
        (key_part, value_part), grad_part = run_backward(
            key_rows[:row_count], value_rows[:row_count], allowed[..., :row_count]
        )
        padding = jnp.zeros(key_part.shape, jnp.float32)
        return (
            (
                jnp.concatenate([key_part, padding], axis=0),
                jnp.concatenate([value_part, padding], axis=0),
            ),
            grad_part,
        )

    (key_acc, value_acc), grad_queries = lax.cond(
        is_noisy, lambda: run_backward(key_rows, value_rows, allowed), backward_own
    )
    returned = shifted(
        jnp.stack(
            [
                key_acc[row_count:].reshape(row_count, model_width),
                value_acc[row_count:].reshape(row_count, model_width),
            ]
        ).astype(jnp.bfloat16),
        "stream",
        -1,
    ).astype(jnp.float32)
    grad_keys = key_acc[:row_count] + returned[0].reshape(row_count, HEADS, HEAD_DIM)
    grad_values = value_acc[:row_count].reshape(row_count, model_width) + returned[1]
    grad_q_turn = rotate_back(grad_queries.reshape(row_count, HEADS, HEAD_DIM), cosine, sine_part)
    grad_k_turn = rotate_back(grad_keys, cosine, sine_part)
    grad_proj = jnp.concatenate(
        [
            grad_q_turn.reshape(row_count, model_width),
            grad_k_turn.reshape(row_count, model_width),
            grad_values,
        ],
        axis=1,
    ).astype(jnp.bfloat16)
    grad_qkv_w = jnp.einsum("td,te->de", first_in, grad_proj, preferred_element_type=jnp.float32)
    grad_first = jnp.einsum("te,de->td", grad_proj, qkv_back, preferred_element_type=jnp.float32)
    grad_in_norm, grad_gain_one = norm_back(
        grad_first, normed_one, inverse_one, gain_back_one.astype(jnp.float32)
    )
    grad_input = (grad_after + grad_in_norm)[None]
    attn_owned = (
        lax.psum_scatter(grad_gain_one, ("seq", "stream"), scatter_dimension=0, tiled=True),
        lax.psum_scatter(grad_qkv_w, ("seq", "stream"), scatter_dimension=0, tiled=True),
        lax.psum_scatter(grad_out_w, ("seq", "stream"), scatter_dimension=0, tiled=True),
    )
    return (
        layer_out,
        grad_input,
        attn_owned[0],
        attn_owned[1],
        attn_owned[2],
        mlp_owned[0],
        mlp_owned[1],
        mlp_owned[2],
        mlp_owned[3],
        mlp_owned[4],
    )


def solution(mesh):
    placed = (
        P("stream", "seq", None),
        P("seq", None),
        P("stream", "seq", None),
        P(("seq", "stream")),
        P(("seq", "stream"), None),
        P(("seq", "stream"), None),
        P(("seq", "stream")),
        P(("seq", "stream"), None),
        P(("seq", "stream")),
        P(("seq", "stream"), None),
        P(("seq", "stream")),
    )
    return jax.shard_map(
        local,
        mesh=mesh,
        in_specs=placed,
        out_specs=(
            P("stream", "seq", None),
            P("stream", "seq", None),
            P(("seq", "stream")),
            P(("seq", "stream"), None),
            P(("seq", "stream"), None),
            P(("seq", "stream")),
            P(("seq", "stream"), None),
            P(("seq", "stream")),
            P(("seq", "stream"), None),
            P(("seq", "stream")),
        ),
        check_vma=False,
    )
```

profile of v0, /device:TPU:0, one launch (start us, length us, event | category | flops | bytes accessed | tf_op | source)
XLA Modules:
  0.0 939.7 jit_solution(3438896426389619557)
XLA Ops:
  13.4 42.3 %all-reduce.11 = (bf16[768]{0:T(1024)(128)(2,1)S(1)}, bf16[768]{0:T(1024)(128)(2,1)}, bf16[768]{0:T(1024)(128)(2,1)S(1)}, bf16[3072]{0:T(1024)(128)(2,1)S(1)}) all-reduce(bf16[768]{0:T(1024)(128)(2,1)S(1)} %dynamic-update-slice, bf16[768]{0:T(1024)(128)(2,1)S(1)} %dynamic-update-slice.3, ...), channel_id=1, replica_groups=mesh['seq'=16,'stream'=2] {'seq','stream'}, use_global_device_ids=true, to_apply=%add.2 | all-reduce | flops 5376 | bytes 21504
  59.8 14.2 %all-gather.5.cloned.1.call-done = bf16[768,2304]{1,0:T(8,128)(2,1)} async-done(((bf16[24,2304]{1,0:T(8,128)(2,1)}), bf16[768,2304]{1,0:T(8,128)(2,1)}) %all-gather.5.cloned.1.call-update) | async-done | bytes 3538960 | tf_op jit(solution)/shard_map/all_gather | solution.py:110
  95.8 30.0 %collective-permute-done = bf16[2,512,768]{2,1,0:T(8,128)(2,1)} collective-permute-done((bf16[2,512,768]{2,1,0:T(8,128)(2,1)}, bf16[2,512,768]{2,1,0:T(8,128)(2,1)}, u32[]{:S(2)}, u32[]{:S(2)}) %collective-permute-start) | collective-permute-done | bytes 1572896 | tf_op jit(solution)/shard_map/ppermute | solution.py:21
  132.8 29.7 %conditional.4 = (f32[1,12,512]{2,1,0:T(8,128)S(1)}, bf16[512,768]{0,1:T(8,128)(2,1)}) conditional(s32[]{:T(128)} %convert_element_type.128, (pred[1,512,1024]{2,1,0:T(8,128)(4,1)}, bf16[1,512,12,64]{1,3,2,0:T(8,128)(2,1)S(1)}, bf16[512,12,64]{0,2,1:T(8,128)(2,1)S(1)}, bf16[1024,12,64]{0,2,1:T(8,128)(2,1)}) %tuple.48, ...), branch_computations={%region_5.8_spmd, %region_8.11_spmd} | conditional | flops 1686497280 | bytes 191037552
  141.0 5.5 fusion.3
  166.6 31.0 %all-gather.9.cloned.1.call-done = bf16[768,3072]{1,0:T(8,128)(2,1)} async-done(((bf16[24,3072]{1,0:T(8,128)(2,1)}), bf16[768,3072]{1,0:T(8,128)(2,1)}) %all-gather.9.cloned.1.call-update) | async-done | bytes 4718608 | tf_op jit(solution)/shard_map/all_gather | solution.py:179
  197.6 8.1 fusion.163
  205.7 57.1 %all-gather.11.cloned.1.call-done = bf16[3072,768]{1,0:T(8,128)(2,1)} async-done(((bf16[96,768]{1,0:T(8,128)(2,1)}), bf16[3072,768]{1,0:T(8,128)(2,1)}) %all-gather.11.cloned.1.call-update) | async-done | bytes 4718608 | tf_op jit(solution)/shard_map/all_gather | solution.py:181
  262.9 9.8 %convert_reduce_fusion = (f32[3072]{0:T(1024)}, bf16[512,3072]{1,0:T(8,128)(2,1)S(1)}) fusion(f32[512,3072]{1,0:T(8,128)} %fusion.163, f32[3072]{0:T(1024)S(1)} %convert_element_type.138, bf16[3072,768]{1,0:T(8,128)(2,1)} %all-gather.11.cloned.1.call-done, bf16[1,512,768]{2,1,0:T(8,128)(2,1)} %param.17), kind=kOutput, calls=%fused_computation.98 | convolution fusion | flops 2452091904 | bytes 14966784 | tf_op jit(solution)/shard_map/td,fd->tf/dot_general | solution.py:208
  282.7 80.5 %conditional.10 = (f32[1024,12,64]{0,2,1:T(8,128)}, f32[1024,12,64]{0,2,1:T(8,128)}, f32[512,12,32]{0,2,1:T(8,128)}, f32[512,12,32]{0,2,1:T(8,128)}) conditional(s32[]{:T(128)} %convert_element_type.128, (pred[1,512,1024]{2,1,0:T(8,128)(4,1)}, bf16[1,512,12,64]{1,3,2,0:T(8,128)(2,1)S(1)}, ...), branch_computations={%region_15.17_spmd.clone.clone, %region_17.19_spmd.clone.clone} | conditional | flops 4190124032 | bytes 211361920 | solution.py:284
  282.7 6.4 fusion.60
  289.0 6.3 fusion.57
  296.2 20.4 %fusion.50 = f32[512,12,64]{0,2,1:T(8,128)} fusion(bf16[512,12,64]{0,2,1:T(8,128)(2,1)S(1)} %get-tuple-element.288, f32[12,512,512]{1,2,0:T(8,128)} %fusion.57, f32[12,512,512]{1,2,0:T(8,128)} %fusion.60, f32[12,512]{1,0:T(8,128)S(1)} %bitcast.196, pred[512,512]{0,1:T(8,128)(4,1)S(1)} %slice_bitcast_fusion.1), kind=kOutput, calls=%fused_computation.45 | convolution fusion | flops 437262848 | bytes 27811840 | tf_op jit(solution)/shard_map/cond/branch_0_fun/while/body/eval_jaxpr/hqk,khd->qhd/dot_general | solution.py:252
  319.4 20.5 %fusion.47 = f32[512,12,64]{0,2,1:T(8,128)} fusion(f32[12,512,512]{1,2,0:T(8,128)} %fusion.57, f32[12,512,512]{1,2,0:T(8,128)} %fusion.60, f32[12,512]{1,0:T(8,128)S(1)} %bitcast.197, pred[512,512]{0,1:T(8,128)(4,1)S(1)} %slice_bitcast_fusion.1, bf16[1,512,12,64]{1,3,2,0:T(8,128)(2,1)S(1)} %get-tuple-element.287), kind=kOutput, calls=%fused_computation.44 | convolution fusion | flops 437262848 | bytes 27811840 | tf_op jit(solution)/shard_map/cond/branch_0_fun/while/body/eval_jaxpr/hqk,qhd->khd/dot_general | solution.py:255
  343.4 6.2 fusion.53
  374.0 84.9 %collective-permute-done.1 = bf16[2,512,768]{1,2,0:T(8,128)(2,1)S(1)} collective-permute-done((bf16[2,512,768]{1,2,0:T(8,128)(2,1)}, bf16[2,512,768]{1,2,0:T(8,128)(2,1)S(1)}, u32[]{:S(2)}, u32[]{:S(2)}) %collective-permute-start.1) | collective-permute-done | bytes 1572896 | tf_op jit(solution)/shard_map/ppermute | solution.py:21
  463.4 5.2 fusion.141
  470.0 7.2 fusion.162
  477.5 10.3 %fusion.143 = f32[3072,768]{1,0:T(8,128)} fusion(bf16[1,512,768]{2,1,0:T(8,128)(2,1)} %param.17, f32[512,3072]{1,0:T(8,128)} %fusion.163, f32[3072]{0:T(1024)S(1)} %convert_element_type.138), kind=kOutput, calls=%fused_computation.152 | convolution fusion | flops 2431647744 | bytes 16527360 | tf_op jit(solution)/shard_map/tf,td->fd/dot_general | solution.py:207
  488.6 9.1 fusion.139
  501.4 40.1 %all-reduce.10 = (f32[768]{0:T(1024)S(1)}, f32[768]{0:T(1024)S(1)}, f32[3072]{0:T(1024)S(1)}, f32[768]{0:T(1024)S(1)}) all-reduce(f32[768]{0:T(1024)S(1)} %get-tuple-element.308, f32[768]{0:T(1024)S(1)} %copy-done.40, f32[3072]{0:T(1024)S(1)} %copy-done.37, ...), channel_id=2, replica_groups=mesh['seq'=16,'stream'=2] {'seq','stream'}, use_global_device_ids=true, to_apply=%region_22.23.clone | all-reduce | flops 5376 | bytes 43008
  547.0 102.4 %reduce-scatter.5.cloned.1.call-done = f32[24,2304]{1,0:T(8,128)} async-done(((f32[768,2304]{1,0:T(8,128)}), f32[24,2304]{1,0:T(8,128)}) %reduce-scatter.5.cloned.1.call-update) | async-done | bytes 221200 | tf_op jit(solution)/shard_map/reduce_scatter | solution.py:317
  649.3 141.1 %reduce-scatter.9.cloned.1.call-done = f32[24,3072]{1,0:T(8,128)} async-done(((f32[768,3072]{1,0:T(8,128)}), f32[24,3072]{1,0:T(8,128)}) %reduce-scatter.9.cloned.1.call-update) | async-done | bytes 294928 | tf_op jit(solution)/shard_map/reduce_scatter | solution.py:220
  790.4 142.2 %reduce-scatter.11.cloned.1.call-done = f32[96,768]{1,0:T(8,128)} async-done(((f32[3072,768]{1,0:T(8,128)}), f32[96,768]{1,0:T(8,128)}) %reduce-scatter.11.cloned.1.call-update) | async-done | bytes 294928 | tf_op jit(solution)/shard_map/reduce_scatter | solution.py:222
  (176 shorter events, 96.8 us)
Async XLA Ops:
  7.2 66.8 %all-gather.5.cloned.1.call-start = ((), (), s32[]{:S(2)}) async-start(), calls=%async_computation.4 | async-start | bytes 3649536 | tf_op jit(solution)/shard_map/all_gather | solution.py:110
  7.9 154.6 %all-gather.7.cloned.1.call-start = ((), (), s32[]{:S(2)}) async-start(), calls=%async_computation.5 | async-start | bytes 1216512 | tf_op jit(solution)/shard_map/all_gather | solution.py:111
  8.7 188.9 %all-gather.9.cloned.1.call-start = ((), (), s32[]{:S(2)}) async-start(), calls=%async_computation.6 | async-start | bytes 4866048 | tf_op jit(solution)/shard_map/all_gather | solution.py:179
  9.4 253.5 %all-gather.11.cloned.1.call-start = ((), (), s32[]{:S(2)}) async-start(), calls=%async_computation.7 | async-start | bytes 4866048 | tf_op jit(solution)/shard_map/all_gather | solution.py:181
  10.0 537.0 %reduce-scatter.7.cloned.1.call-start = ((), (), s32[]{:S(2)}) async-start(), calls=%async_computation.9 | async-start | bytes 2433024 | tf_op jit(solution)/shard_map/reduce_scatter | solution.py:318
  55.7 22.7 %copy-start.34 = (f32[768]{0:T(1024)}, f32[768]{0:T(1024)S(1)}, u32[]{:S(2)}) copy-start(f32[768]{0:T(1024)S(1)} %convert_element_type.130) | copy-start | bytes 9220
  57.9 20.5 %copy-start.32 = (f32[512]{0:T(512)}, f32[512]{0:T(512)S(1)}, u32[]{:S(2)}) copy-start(f32[512]{0:T(512)S(1)} %broadcast_multiply_fusion.5) | copy-start | bytes 6148
  59.5 19.0 %copy-start.38 = (f32[512]{0:T(512)}, f32[512]{0:T(512)S(1)}, u32[]{:S(2)}) copy-start(f32[512]{0:T(512)S(1)} %add_rsqrt_fusion.1) | copy-start | bytes 6148
  59.8 35.7 %copy-start.21 = (f32[512,32]{0,1:T(8,128)}, f32[512,32]{0,1:T(8,128)S(1)}, u32[]{:S(2)}) copy-start(f32[512,32]{0,1:T(8,128)S(1)} %get-tuple-element.348) | copy-start | bytes 196612
  59.8 35.7 %copy-start.23 = (f32[512,32]{0,1:T(8,128)}, f32[512,32]{0,1:T(8,128)S(1)}, u32[]{:S(2)}) copy-start(f32[512,32]{0,1:T(8,128)S(1)} %get-tuple-element.349) | copy-start | bytes 196612
  84.9 40.9 %collective-permute-start = (bf16[2,512,768]{2,1,0:T(8,128)(2,1)}, bf16[2,512,768]{2,1,0:T(8,128)(2,1)}, u32[]{:S(2)}, u32[]{:S(2)}) collective-permute-start(bf16[2,512,768]{2,1,0:T(8,128)(2,1)} %pad_maximum_fusion.1), channel_id=1, source_target_pairs={{0,1},{2,3},{4,5},{6,7},{8,9},{10,11},{12,13},{14,15},{16,17},{18,... | collective-permute-start | bytes 4718600 | tf_op jit(solution)/shard_map/ppermute | solution.py:21
  262.9 9.8 %copy-start.7 = (f32[512,768]{1,0:T(8,128)S(1)}, f32[512,768]{1,0:T(8,128)}, u32[]{:S(2)}) copy-start(f32[512,768]{1,0:T(8,128)} %copy-done.6) | copy-start | bytes 4718596
  262.9 9.8 %copy-start.42 = (bf16[768,3072]{1,0:T(8,128)(2,1)S(1)}, bf16[768,3072]{1,0:T(8,128)(2,1)}, u32[]{:S(2)}) copy-start(bf16[768,3072]{1,0:T(8,128)(2,1)} %all-gather.9.cloned.1.call-done) | copy-start | bytes 14155780
  367.6 91.3 %collective-permute-start.1 = (bf16[2,512,768]{1,2,0:T(8,128)(2,1)}, bf16[2,512,768]{1,2,0:T(8,128)(2,1)S(1)}, u32[]{:S(2)}, u32[]{:S(2)}) collective-permute-start(bf16[2,512,768]{1,2,0:T(8,128)(2,1)} %pad_maximum_fusion.4), channel_id=1, source_target_pairs={{1,0},{3,2},{5,4},{7,6},{9,8},{11,10},{13,12},{15,14},{17,16},{19,... | collective-permute-start | bytes 4718600 | tf_op jit(solution)/shard_map/ppermute | solution.py:21
  372.4 276.9 %reduce-scatter.5.cloned.1.call-start = ((), (), s32[]{:S(2)}) async-start(), calls=%async_computation.8 | async-start | bytes 7299072 | tf_op jit(solution)/shard_map/reduce_scatter | solution.py:317
  374.0 85.6 %copy-start.15 = (f32[1024,12,64]{0,2,1:T(8,128)S(1)}, f32[1024,12,64]{0,2,1:T(8,128)}, u32[]{:S(2)}) copy-start(f32[1024,12,64]{0,2,1:T(8,128)} %get-tuple-element.216) | copy-start | bytes 9437188
  468.7 321.7 %reduce-scatter.9.cloned.1.call-start = ((), (), s32[]{:S(2)}) async-start(), calls=%async_computation.10 | async-start | bytes 9732096 | tf_op jit(solution)/shard_map/reduce_scatter | solution.py:220
  477.2 455.4 %reduce-scatter.11.cloned.1.call-start = ((), (), s32[]{:S(2)}) async-start(), calls=%async_computation.11 | async-start | bytes 9732096 | tf_op jit(solution)/shard_map/reduce_scatter | solution.py:222
  488.6 9.2 copy-start.17
  488.6 9.2 copy-start.26
  488.6 9.2 copy-start.28
  488.6 9.2 copy-start.31
  488.6 9.2 copy-start.43
  497.8 46.0 %copy-start.18 = (bf16[1,512,768]{2,1,0:T(8,128)(2,1)S(1)}, bf16[1,512,768]{2,1,0:T(8,128)(2,1)}, u32[]{:S(2)}) copy-start(bf16[1,512,768]{2,1,0:T(8,128)(2,1)} %param.15) | copy-start | bytes 2359300
  (24 other events, 62.8 us)
Sparse Core Ops, SparseCore 0:
  10.9 63.0 all-gather.4
  76.9 53.6 all-gather.6
  133.6 63.9 all-gather.8
  200.4 62.4 all-gather.10
  372.5 151.5 reduce-scatter.6
  531.1 118.1 reduce-scatter.4
  655.8 134.5 reduce-scatter.8
  797.9 134.7 reduce-scatter.10
where the time goes:
time: 947 us; the launch traced here: 940 us
  waiting for transfers between devices  606 us (64%)
  matrix products  136 us (14%)
  blocking collectives  82.3 us (9%)
  local copies, waits for them, and re-layouts  44.1 us (5%)
  loops' own time  27.7 us (3%)
  other arithmetic  22.4 us (2%)
  between operations  15 us (2%)
    reduce_scatter x1, waiting for transfers between devices, local(): lax.psum_scatter(grad_down_w, ('seq', 'stream'), scatter_dimension=0, til...  142 us
    reduce_scatter x1, waiting for transfers between devices, local(): lax.psum_scatter(grad_up_w, ('seq', 'stream'), scatter_dimension=0, tiled...  141 us
    ppermute x2, waiting for transfers between devices, shifted(): return lax.ppermute(block, axis, route)  115 us
    reduce_scatter x1, waiting for transfers between devices, local(): lax.psum_scatter(grad_qkv_w, ('seq', 'stream'), scatter_dimension=0, tile...  102 us
    unnamed x2, blocking collectives  82.3 us
    all_gather x1, waiting for transfers between devices, local(): lax.all_gather(down_weight, ('seq', 'stream'), axis=0, tiled=True)  57.1 us
    all_gather x1, waiting for transfers between devices, local(): lax.all_gather(up_weight, ('seq', 'stream'), axis=0, tiled=True)  31 us
    dot_general x1, matrix products, attend_back(): jnp.einsum('hqk,qhd->khd', grad_scores, query_block, preferred_element_ty...  20.5 us
  transfers between devices with their start and end apart: 10, of which 8 were waited for; matrix products, arithmetic and copies ran while one was open for 11% of the time, Pallas kernels for 0%

commit v1 on v0

--- a/solution.py
+++ b/solution.py
@@ -4,6 +4,8 @@
 import jax
 import jax.numpy as jnp
 from jax import lax
+from jax.experimental import pallas as pl
+from jax.experimental.pallas import tpu as pltpu
 from jax.sharding import PartitionSpec as P
 
 HEADS = 12
@@ -21,8 +23,118 @@
     return lax.ppermute(block, axis, route)
 
 
+ALL = ("seq", "stream")
+STREAM_BIT, CORE_BIT, NEAR_BIT = 1, 2, 4
+
+
+def device_count():
+    return lax.axis_size("seq") * lax.axis_size("stream")
+
+
+def far_groups():
+    bits = []
+    bit = 2 * NEAR_BIT
+    while bit < device_count():
+        bits.append(bit)
+        bit *= 2
+    groups = []
+    while bits:
+        taken, bits = bits[:2], bits[2:]
+        groups.append(taken if len(taken) == 1 else [taken[0], taken[1], taken[0] + taken[1]])
+    return groups
+
+
+def flip(block, mask):
+    return lax.ppermute(block, ALL, [(i, i ^ mask) for i in range(device_count())])
+
+
+def place(pieces, keys, me):
+    total = sum(len(k) for k in keys)
+    shape = (total,) + pieces[0].shape[1:]
+
+    def body(me_ref, *refs):
+        out, sem = refs[-2], refs[-1]
+        for piece, key in zip(refs[:-2], keys):
+            for j, rel in enumerate(key):
+                pltpu.make_async_copy(piece.at[j], out.at[me_ref[0] ^ rel], sem).start()
+        pltpu.make_async_copy(out, out, sem).wait()
+
+    return pl.pallas_call(
+        body,
+        out_shape=jax.ShapeDtypeStruct(shape, pieces[0].dtype),
+        in_specs=[pl.BlockSpec(memory_space=pltpu.SMEM)]
+        + [pl.BlockSpec(memory_space=pl.ANY)] * len(pieces),
+        out_specs=pl.BlockSpec(memory_space=pltpu.VMEM),
+        scratch_shapes=[pltpu.SemaphoreType.DMA],
+    )(me, *pieces)
+
+
+def gather(shard, near_order, me):
+    piece, key = shard[None], [0]
+    for group in far_groups():
+        got = [piece] + [flip(piece, mask) for mask in group]
+        key = [k ^ mask for mask in [0] + group for k in key]
+        piece = jnp.concatenate(got, axis=0)
+    pieces, keys = [piece], [key]
+    for bit in near_order + (CORE_BIT,):
+        pieces = pieces + [flip(p, bit) for p in pieces]
+        keys = keys + [[k ^ bit for k in key] for key in keys]
+    return place(pieces, keys, me)
+
+
+def spread(whole, orders, me):
+    def body(me_ref, src, *refs):
+        sem = refs[-1]
+        for out, order in zip(refs[:-1], orders):
+            for j, rel in enumerate(order):
+                pltpu.make_async_copy(src.at[me_ref[0] ^ rel], out.at[j], sem).start()
+        pltpu.make_async_copy(src, src, sem).wait()
+
+    return pl.pallas_call(
+        body,
+        out_shape=[
+            jax.ShapeDtypeStruct((len(order),) + whole.shape[1:], whole.dtype) for order in orders
+        ],
+        in_specs=[pl.BlockSpec(memory_space=pltpu.SMEM), pl.BlockSpec(memory_space=pltpu.VMEM)],
+        out_specs=[pl.BlockSpec(memory_space=pl.ANY)] * len(orders),
+        scratch_shapes=[pltpu.SemaphoreType.DMA],
+    )(me, whole)
+
+
+def scatter_sum(whole, near_order, me):
+    kind = whole.dtype
+    order = [0]
+    for group in far_groups():
+        order = [k ^ mask for mask in [0] + group for k in order]
+    for bit in reversed(near_order):
+        order = [k ^ b for b in (0, bit) for k in order]
+    keep, send = spread(whole, [order, [k ^ CORE_BIT for k in order]], me)
+    total = keep.astype(jnp.float32) + flip(send, CORE_BIT).astype(jnp.float32)
+    for bit in near_order:
+        half = total.shape[0] // 2
+        recv = flip(total[half:].astype(kind), bit)
+        total = total[:half] + recv.astype(jnp.float32)
+    for group in reversed(far_groups()):
+        part = total.shape[0] // (len(group) + 1)
+        recv = [
+            flip(total[(i + 1) * part : (i + 2) * part].astype(kind), mask)
+            for i, mask in enumerate(group)
+        ]
+        total = total[:part]
+        for r in recv:
+            total = total + r.astype(jnp.float32)
+    return total[0]
+
+
+ORDER_A = (STREAM_BIT, NEAR_BIT)
+ORDER_B = (NEAR_BIT, STREAM_BIT)
+
+
 def doc_layout(pack_lengths, row_count):
-    seq_ends = jnp.cumsum(pack_lengths)
+    ends = [pack_lengths[0]]
+    for i in range(1, pack_lengths.shape[0]):
+        ends.append(ends[-1] + pack_lengths[i])
+    seq_ends = jnp.stack(ends)
     row_index = jnp.arange(row_count, dtype=jnp.int32)
     passed = seq_ends[None, :] <= row_index[:, None]
     doc_ids = jnp.sum(passed.astype(jnp.int32), axis=1)
@@ -105,12 +217,22 @@
     head_scale = HEAD_DIM ** (-0.5)
     block_rows = min(512, row_count)
     block_count = row_count // block_rows
-    attn_set = (
-        lax.all_gather(attn_gain, ("seq", "stream"), axis=0, tiled=True),
-        lax.all_gather(qkv_weight, ("seq", "stream"), axis=0, tiled=True),
-        lax.all_gather(out_weight, ("seq", "stream"), axis=0, tiled=True),
-    )
-    gain_one, qkv_full, out_full = attn_set
+    me_flat = (lax.axis_index("seq") * 2 + lax.axis_index("stream")).astype(jnp.int32)
+    me = me_flat[None]
+    n_dev = device_count()
+    small_sizes = (attn_gain.shape[0], mlp_gain.shape[0], down_bias.shape[0], up_bias.shape[0])
+    small = jnp.concatenate([attn_gain, mlp_gain, down_bias, up_bias])
+    small_width = -(-small.shape[0] // 128) * 128
+    small = jnp.pad(small, (0, small_width - small.shape[0])).reshape(1, small_width)
+    small_all = gather(small, ORDER_A, me).reshape(n_dev, small_width)
+
+    def small_part(i):
+        start = sum(small_sizes[:i])
+        return small_all[:, start : start + small_sizes[i]].reshape(-1)
+
+    gain_one = small_part(0)
+    qkv_full = gather(qkv_weight, ORDER_A, me).reshape(-1, qkv_weight.shape[1])
+    out_full = gather(out_weight, ORDER_B, me).reshape(-1, out_weight.shape[1])
     resid_in = tokens[0].astype(jnp.float32)
     first_full, normed_one, inverse_one = norm_rows(resid_in, gain_one.astype(jnp.float32))
     first_in = first_full.astype(jnp.bfloat16)
@@ -174,14 +296,9 @@
     )
     attn_low = attn_rows.reshape(row_count, model_width).astype(jnp.bfloat16)
     after_attn = resid_in + jnp.dot(attn_low, out_full, preferred_element_type=jnp.float32)
-    mlp_set = (
-        lax.all_gather(mlp_gain, ("seq", "stream"), axis=0, tiled=True),
-        lax.all_gather(up_weight, ("seq", "stream"), axis=0, tiled=True),
-        lax.all_gather(up_bias, ("seq", "stream"), axis=0, tiled=True),
-        lax.all_gather(down_weight, ("seq", "stream"), axis=0, tiled=True),
-        lax.all_gather(down_bias, ("seq", "stream"), axis=0, tiled=True),
-    )
-    gain_two, up_full, up_bias_full, down_full, down_bias_full = mlp_set
+    up_full = gather(up_weight, ORDER_B, me).reshape(-1, up_weight.shape[1])
+    down_full = gather(down_weight, ORDER_A, me).reshape(-1, down_weight.shape[1])
+    gain_two, down_bias_full, up_bias_full = small_part(1), small_part(2), small_part(3)
     second_full, normed_two, inverse_two = norm_rows(after_attn, gain_two.astype(jnp.float32))
     second_in = second_full.astype(jnp.bfloat16)
     pre_act = jnp.dot(second_in, up_full, preferred_element_type=jnp.float32) + up_bias_full.astype(
@@ -194,14 +311,7 @@
         + down_bias_full.astype(jnp.float32)
     )
     layer_out = layer_full.astype(jnp.bfloat16)[None]
-    mlp_back = (
-        lax.all_gather(mlp_gain, ("seq", "stream"), axis=0, tiled=True),
-        lax.all_gather(up_weight, ("seq", "stream"), axis=0, tiled=True),
-        lax.all_gather(up_bias, ("seq", "stream"), axis=0, tiled=True),
-        lax.all_gather(down_weight, ("seq", "stream"), axis=0, tiled=True),
-        lax.all_gather(down_bias, ("seq", "stream"), axis=0, tiled=True),
-    )
-    gain_back_two, up_back, _, down_back, _ = mlp_back
+    gain_back_two, up_back, down_back = gain_two, up_full, down_full
     grad_top = cotangent[0]
     grad_down_bias = jnp.sum(grad_top, axis=0, dtype=jnp.float32)
     grad_down_w = jnp.einsum("tf,td->fd", activated, grad_top, preferred_element_type=jnp.float32)
@@ -215,19 +325,13 @@
         grad_second, normed_two, inverse_two, gain_back_two.astype(jnp.float32)
     )
     grad_after = grad_top.astype(jnp.float32) + grad_mid
-    mlp_owned = (
-        lax.psum_scatter(grad_gain_two, ("seq", "stream"), scatter_dimension=0, tiled=True),
-        lax.psum_scatter(grad_up_w, ("seq", "stream"), scatter_dimension=0, tiled=True),
-        lax.psum_scatter(grad_up_b, ("seq", "stream"), scatter_dimension=0, tiled=True),
-        lax.psum_scatter(grad_down_w, ("seq", "stream"), scatter_dimension=0, tiled=True),
-        lax.psum_scatter(grad_down_bias, ("seq", "stream"), scatter_dimension=0, tiled=True),
-    )
-    attn_back = (
-        lax.all_gather(attn_gain, ("seq", "stream"), axis=0, tiled=True),
-        lax.all_gather(qkv_weight, ("seq", "stream"), axis=0, tiled=True),
-        lax.all_gather(out_weight, ("seq", "stream"), axis=0, tiled=True),
-    )
-    gain_back_one, qkv_back, out_back = attn_back
+    owned_up = scatter_sum(
+        grad_up_w.astype(jnp.bfloat16).reshape(n_dev, -1, grad_up_w.shape[1]), ORDER_B, me
+    )
+    owned_down = scatter_sum(
+        grad_down_w.astype(jnp.bfloat16).reshape(n_dev, -1, grad_down_w.shape[1]), ORDER_A, me
+    )
+    gain_back_one, qkv_back, out_back = gain_one, qkv_full, out_full
     grad_attn_low = grad_after.astype(jnp.bfloat16)
     grad_out_w = jnp.einsum(
         "td,te->de", attn_low, grad_attn_low, preferred_element_type=jnp.float32
@@ -312,22 +416,37 @@
         grad_first, normed_one, inverse_one, gain_back_one.astype(jnp.float32)
     )
     grad_input = (grad_after + grad_in_norm)[None]
-    attn_owned = (
-        lax.psum_scatter(grad_gain_one, ("seq", "stream"), scatter_dimension=0, tiled=True),
-        lax.psum_scatter(grad_qkv_w, ("seq", "stream"), scatter_dimension=0, tiled=True),
-        lax.psum_scatter(grad_out_w, ("seq", "stream"), scatter_dimension=0, tiled=True),
-    )
+    owned_qkv = scatter_sum(
+        grad_qkv_w.astype(jnp.bfloat16).reshape(n_dev, -1, grad_qkv_w.shape[1]), ORDER_A, me
+    )
+    owned_out = scatter_sum(
+        grad_out_w.astype(jnp.bfloat16).reshape(n_dev, -1, grad_out_w.shape[1]), ORDER_B, me
+    )
+    small_grad = jnp.concatenate(
+        [
+            g.reshape(n_dev, -1)
+            for g in (grad_gain_one, grad_gain_two, grad_down_bias, grad_up_b)
+        ],
+        axis=1,
+    )
+    small_grad = jnp.pad(small_grad, ((0, 0), (0, small_width - small_grad.shape[1])))
+    owned_small = scatter_sum(small_grad.reshape(n_dev, 1, small_width), ORDER_A, me)[0]
+
+    def small_owned(i):
+        start = sum(small_sizes[:i])
+        return owned_small[start : start + small_sizes[i]]
+
     return (
         layer_out,
         grad_input,
-        attn_owned[0],
-        attn_owned[1],
-        attn_owned[2],
-        mlp_owned[0],
-        mlp_owned[1],
-        mlp_owned[2],
-        mlp_owned[3],
-        mlp_owned[4],
+        small_owned(0),
+        owned_qkv,
+        owned_out,
+        small_owned(1),
+        owned_up,
+        small_owned(3),
+        owned_down,
+        small_owned(2),
     )
 
 

time: 947 us -> 572 us (0.60)
  waiting for transfers between devices: 606 us -> 138 us
  starting transfers between devices: 6.33 us -> 141 us
  blocking collectives: 82.3 us -> 0 us
  Pallas kernels: 0 us -> 33.5 us
  other arithmetic: 22.4 us -> 47.5 us
  loops' own time: 27.7 us -> 11.3 us
  between operations: 15 us -> 5.1 us
    reduce_scatter x4 -> x0, waiting for transfers between devices: 386 us -> none  [the longest x1 142 us: local(): lax.psum_scatter(grad_down_w, ('seq', 'stream'), scatter_dimension=0, til...]
    ppermute x0 -> x80, starting transfers between devices: none -> 135 us  [flip(): lax.ppermute(block, ALL, [(i, i ^ mask) for i in range(device_count())])]
    ppermute x0 -> x80, waiting for transfers between devices: none -> 127 us  [flip(): lax.ppermute(block, ALL, [(i, i ^ mask) for i in range(device_count())])]
    ppermute x2, waiting for transfers between devices: 115 us -> 10.7 us  [shifted(): return lax.ppermute(block, axis, route)]
    all_gather x4 -> x0, waiting for transfers between devices: 102 us -> none  [the longest x1 57.1 us: local(): lax.all_gather(down_weight, ('seq', 'stream'), axis=0, tiled=True)]
    unnamed x2 -> x0, blocking collectives: 82.3 us -> none
    pallas_call x0 -> x10, Pallas kernels: none -> 33.5 us  [the longest x5 16.8 us: place(): pl.pallas_call(body, out_shape=jax.ShapeDtypeStruct(shape, pieces[0].dtyp...]
    unnamed x1 -> x0, loops' own time: 16.2 us -> none
  transfers between devices with their start and end apart: 10 -> 82, of which waited for: 8 -> 23; matrix products, arithmetic and copies ran while one was open for 11% -> 30% of each run, Pallas kernels for 0% -> 6%
where the time goes in v1:
time: 572 us; the launch traced here: 564 us
  starting transfers between devices  141 us (25%)
  matrix products  139 us (24%)
  waiting for transfers between devices  138 us (24%)
  local copies, waits for them, and re-layouts  48.7 us (9%)
  other arithmetic  47.5 us (8%)
  Pallas kernels  33.5 us (6%)
  loops' own time  11.3 us (2%)
    ppermute x80, starting transfers between devices, flip(): lax.ppermute(block, ALL, [(i, i ^ mask) for i in range(device_count())])  135 us
    ppermute x80, waiting for transfers between devices, flip(): lax.ppermute(block, ALL, [(i, i ^ mask) for i in range(device_count())])  127 us
    dot_general x1, matrix products, attend_back(): jnp.einsum('hqk,qhd->khd', grad_scores, query_block, preferred_element_ty...  20.8 us
    dot_general x1, matrix products, attend_back(): jnp.einsum('hqk,khd->qhd', grad_scores, key_set, preferred_element_type=j...  20.3 us
    dot_general x1, matrix products, local(): jnp.dot(second_in, up_full, preferred_element_type=jnp.float32)  18.1 us
    pallas_call x5, Pallas kernels, place(): pl.pallas_call(body, out_shape=jax.ShapeDtypeStruct(shape, pieces[0].dtyp...  16.8 us
    pallas_call x5, Pallas kernels, spread(): pl.pallas_call(body, out_shape=[jax.ShapeDtypeStruct((len(order),) + whol...  16.6 us
  transfers between devices with their start and end apart: 82, of which 23 were waited for; matrix products, arithmetic and copies ran while one was open for 30% of the time, Pallas kernels for 6%

profile of v1, /device:TPU:0, one launch (start us, length us, event | category | flops | bytes accessed | tf_op | source)
XLA Modules:
  0.0 564.3 jit_solution(9944849652426719249)
XLA Ops:
  44.9 6.3 %collective-permute-done.32 = bf16[1,24,3072]{2,1,0:T(8,128)(2,1)S(1)} collective-permute-done((bf16[1,24,3072]{2,1,0:T(8,128)(2,1)}, bf16[1,24,3072]{2,1,0:T(8,128)(2,1)S(1)}, u32[]{:S(2)}, u32[]{:S(2)}) %collective-permute-start.32) | collective-permute-done | bytes 147488 | tf_op jit(solution)/shard_map/ppermute | solution.py:48
  54.2 9.7 %collective-permute-done.42 = bf16[1,96,768]{2,1,0:T(8,128)(2,1)} collective-permute-done((bf16[1,96,768]{2,1,0:T(8,128)(2,1)}, bf16[1,96,768]{2,1,0:T(8,128)(2,1)}, u32[]{:S(2)}, u32[]{:S(2)}) %collective-permute-start.42) | collective-permute-done | bytes 147488 | tf_op jit(solution)/shard_map/ppermute | solution.py:48
  100.7 7.4 %collective-permute-done.44.refs_1_ = bf16[4,96,768]{2,1,0:T(8,128)(2,1)} collective-permute-done((bf16[4,96,768]{2,1,0:T(8,128)(2,1)}, bf16[4,96,768]{2,1,0:T(8,128)(2,1)}, u32[]{:S(2)}, u32[]{:S(2)}) %collective-permute-start.44) | collective-permute-done | bytes 589856 | tf_op jit(solution)/shard_map/ppermute | solution.py:48
  109.0 10.9 %collective-permute-done.36.refs_3_ = bf16[4,24,3072]{2,1,0:T(8,128)(2,1)} collective-permute-done((bf16[4,24,3072]{2,1,0:T(8,128)(2,1)}, bf16[4,24,3072]{2,1,0:T(8,128)(2,1)}, u32[]{:S(2)}, u32[]{:S(2)}) %collective-permute-start.36) | collective-permute-done | bytes 589856 | tf_op jit(solution)/shard_map/ppermute | solution.py:48
  142.0 10.7 %collective-permute-done.20 = bf16[2,512,768]{2,1,0:T(8,128)(2,1)} collective-permute-done((bf16[2,512,768]{2,1,0:T(8,128)(2,1)}, bf16[2,512,768]{2,1,0:T(8,128)(2,1)}, u32[]{:S(2)}, u32[]{:S(2)}) %collective-permute-start.20) | collective-permute-done | bytes 1572896 | tf_op jit(solution)/shard_map/ppermute | solution.py:23
  159.7 13.9 %conditional.2 = (f32[1,12,512]{2,1,0:T(8,128)S(1)}, bf16[512,768]{0,1:T(8,128)(2,1)}) conditional(s32[]{:T(128)} %convert_element_type.280, (pred[1,512,1024]{2,1,0:T(8,128)(4,1)}, bf16[1,512,12,64]{1,3,2,0:T(8,128)(2,1)S(1)}, bf16[512,12,64]{0,2,1:T(8,128)(2,1)S(1)}, bf16[1024,12,64]{0,2,1:T(8,128)(2,1)}) %tuple.38, ...), branch_computations={%region_4.7_spmd, %region_7.10_spmd} | conditional | flops 1686497280 | bytes 191037552 | solution.py:292
  167.6 5.5 fusion.3
  176.7 18.1 %fusion.190 = f32[512,3072]{1,0:T(8,128)S(1)} fusion(bf16[768,3072]{1,0:T(8,128)(2,1)} %bitcast.239, f32[512,768]{1,0:T(8,128)S(1)} %get-tuple-element.380, f32[768]{0:T(1024)S(1)} %reshape.434, f32[512]{0:T(512)S(1)} %add_rsqrt_fusion, f32[512]{0:T(512)S(1)} %broadcast_multiply_fusion.4), kind=kOutput, calls=%fused_computation.282 | convolution fusion | flops 2417491968 | bytes 12590080 | tf_op jit(solution)/shard_map/dot_general | solution.py:304
  194.9 7.2 %convert_reduce_fusion = (f32[3072]{0:T(1024)}, bf16[512,3072]{1,0:T(8,128)(2,1)S(1)}) fusion(f32[512,3072]{1,0:T(8,128)S(1)} %fusion.190, f32[3072]{0:T(1024)S(1)} %reshape.435, bf16[3072,768]{1,0:T(8,128)(2,1)S(1)} %bitcast.238, bf16[1,512,768]{2,1,0:T(8,128)(2,1)S(1)} %copy-done.37), kind=kOutput, calls=%fused_computation.103 | convolution fusion | flops 2452091904 | bytes 14966784 | tf_op jit(solution)/shard_map/td,fd->tf/dot_general | solution.py:318
  213.3 9.0 %convolution_convert_fusion = bf16[3072,768]{1,0:T(8,128)(2,1)} fusion(bf16[1,512,768]{2,1,0:T(8,128)(2,1)} %param.17, f32[512,3072]{1,0:T(8,128)} %copy-done.75, f32[3072]{0:T(1024)S(1)} %reshape.435), kind=kOutput, calls=%fused_computation.105 | convolution fusion | flops 2434007040 | bytes 11808768 | tf_op jit(solution)/shard_map/tf,td->fd/dot_general | solution.py:317
  233.4 80.3 %conditional.3 = (f32[1024,12,64]{0,2,1:T(8,128)}, f32[1024,12,64]{0,2,1:T(8,128)}, f32[512,12,32]{0,2,1:T(8,128)}, f32[512,12,32]{0,2,1:T(8,128)}) conditional(s32[]{:T(128)} %convert_element_type.280, (pred[1,512,1024]{2,1,0:T(8,128)(4,1)}, bf16[1,512,12,64]{1,3,2,0:T(8,128)(2,1)S(1)}, ...), branch_computations={%region_14.16_spmd.clone.clone, %region_16.18_spmd.clone.clone} | conditional | flops 4190124032 | bytes 211361920 | solution.py:388
  233.4 6.4 %fusion.60 = f32[12,512,512]{1,2,0:T(8,128)} fusion(bf16[512,12,64]{0,2,1:T(8,128)(2,1)S(1)} %get-tuple-element.290, bf16[1,512,12,64]{1,3,2,0:T(8,128)(2,1)S(1)} %get-tuple-element.289), kind=kOutput, calls=%fused_computation.52 | convolution fusion | flops 402653184 | bytes 14155776 | tf_op jit(solution)/shard_map/cond/branch_0_fun/while/body/eval_jaxpr/qhd,khd->hqk/dot_general | solution.py:271
  239.9 6.4 %fusion.57 = f32[12,512,512]{1,2,0:T(8,128)} fusion(bf16[1,512,12,64]{1,3,2,0:T(8,128)(2,1)S(1)} %copy-done.12, bf16[1024,12,64]{0,2,1:T(8,128)(2,1)S(1)} %copy-done.2), kind=kOutput, calls=%fused_computation.49 | convolution fusion | flops 402653184 | bytes 14155776 | tf_op jit(solution)/shard_map/cond/branch_0_fun/while/body/eval_jaxpr/qhd,khd->hqk/dot_general | solution.py:351
  247.2 20.3 %fusion.50 = f32[512,12,64]{0,2,1:T(8,128)} fusion(bf16[512,12,64]{0,2,1:T(8,128)(2,1)S(1)} %get-tuple-element.290, f32[12,512,512]{1,2,0:T(8,128)} %fusion.57, f32[12,512,512]{1,2,0:T(8,128)} %fusion.60, f32[12,512]{1,0:T(8,128)S(1)} %bitcast.277, pred[512,512]{0,1:T(8,128)(4,1)S(1)} %slice_bitcast_fusion.1), kind=kOutput, calls=%fused_computation.45 | convolution fusion | flops 437262848 | bytes 27811840 | tf_op jit(solution)/shard_map/cond/branch_0_fun/while/body/eval_jaxpr/hqk,khd->qhd/dot_general | solution.py:356
  270.2 20.8 %fusion.47 = f32[512,12,64]{0,2,1:T(8,128)} fusion(f32[12,512,512]{1,2,0:T(8,128)} %fusion.57, f32[12,512,512]{1,2,0:T(8,128)} %fusion.60, f32[12,512]{1,0:T(8,128)S(1)} %bitcast.278, pred[512,512]{0,1:T(8,128)(4,1)S(1)} %slice_bitcast_fusion.1, bf16[1,512,12,64]{1,3,2,0:T(8,128)(2,1)S(1)} %get-tuple-element.289), kind=kOutput, calls=%fused_computation.44 | convolution fusion | flops 437262848 | bytes 27811840 | tf_op jit(solution)/shard_map/cond/branch_0_fun/while/body/eval_jaxpr/hqk,qhd->khd/dot_general | solution.py:359
  294.6 6.1 %fusion.53 = f32[512,12,64]{0,2,1:T(8,128)S(1)} fusion(f32[12,512,512]{1,2,0:T(8,128)} %fusion.60, f32[12,512]{1,0:T(8,128)S(1)} %bitcast.279, pred[512,512]{0,1:T(8,128)(4,1)S(1)} %slice_bitcast_fusion.1, bf16[1,512,12,64]{1,3,2,0:T(8,128)(2,1)S(1)} %copy-done.12), kind=kOutput, calls=%fused_computation.46 | convolution fusion | flops 415236096 | bytes 15228928 | tf_op jit(solution)/shard_map/cond/branch_0_fun/while/body/eval_jaxpr/hqk,qhd->khd/dot_general | solution.py:362
  320.7 67.0 %collective-permute-start.66 = (bf16[4,24,768]{2,1,0:T(8,128)(2,1)S(1)}, bf16[4,24,768]{2,1,0:T(8,128)(2,1)S(1)}, u32[]{:S(2)}, u32[]{:S(2)}) collective-permute-start(bf16[4,24,768]{2,1,0:T(8,128)(2,1)S(1)} %slice.541), channel_id=1, source_target_pairs={{0,1},{1,0},{2,3},{3,2},{4,5},{5,4},{6,7},{7,6},{8,9},{9,8},{10,11... | collective-permute-start | bytes 442376 | tf_op jit(solution)/shard_map/ppermute | solution.py:48
  387.6 9.0 %fusion.145 = bf16[1,512,768]{2,1,0:T(8,128)(2,1)} fusion(f32[512,768]{1,0:T(8,128)S(1)} %copy-done.19, bf16[3072,768]{1,0:T(8,128)(2,1)} %bitcast.235, f32[768]{0:T(1024)S(1)} %copy-done.65, f32[512,3072]{1,0:T(8,128)} %copy-done.75, f32[3072]{0:T(1024)S(1)} %reshape.435), kind=kOutput, calls=%fused_computation.167 | convolution fusion | flops 2432827392 | bytes 13384704 | tf_op jit(solution)/shard_map/dot_general | solution.py:310
  396.6 27.0 %collective-permute-done.66 = bf16[4,24,768]{2,1,0:T(8,128)(2,1)S(1)} collective-permute-done((bf16[4,24,768]{2,1,0:T(8,128)(2,1)S(1)}, bf16[4,24,768]{2,1,0:T(8,128)(2,1)S(1)}, u32[]{:S(2)}, u32[]{:S(2)}) %collective-permute-start.66) | collective-permute-done | bytes 147488 | tf_op jit(solution)/shard_map/ppermute | solution.py:48
  457.2 5.7 %convolution_convert_fusion.2 = bf16[768,2304]{1,0:T(8,128)(2,1)} fusion(bf16[512,768]{0,1:T(8,128)(2,1)} %copy-done.38, bf16[512,768]{0,1:T(8,128)(2,1)} %bitcast.258, bf16[512,768]{0,1:T(8,128)(2,1)S(1)} %bitcast.256, bf16[1,512,768]{2,1,0:T(8,128)(2,1)S(1)} %copy-done.17, f32[768]{0:T(1024)S(1)} %copy-done.58, f32[512]{0:T(512)S(1)} %copy-done.62, ...), kind=kOutput, calls=%fused_computation.107 | convolution fusion | flops 1822752768 | bytes 6691840 | tf_op jit(solution)/shard_map/td,te->de/dot_general | solution.py:413
  493.5 9.3 %collective-permute-done.77 = bf16[8,96,768]{2,1,0:T(8,128)(2,1)} collective-permute-done((bf16[8,96,768]{2,1,0:T(8,128)(2,1)S(1)}, bf16[8,96,768]{2,1,0:T(8,128)(2,1)}, u32[]{:S(2)}, u32[]{:S(2)}) %collective-permute-start.77) | collective-permute-done | bytes 1179680 | tf_op jit(solution)/shard_map/ppermute | solution.py:48
  506.6 7.1 %collective-permute-done.71 = bf16[8,24,3072]{2,1,0:T(8,128)(2,1)} collective-permute-done((bf16[8,24,3072]{2,1,0:T(8,128)(2,1)}, bf16[8,24,3072]{2,1,0:T(8,128)(2,1)}, u32[]{:S(2)}, u32[]{:S(2)}) %collective-permute-start.71) | collective-permute-done | bytes 1179680 | tf_op jit(solution)/shard_map/ppermute | solution.py:48
  524.4 8.0 %collective-permute-done.72 = bf16[4,24,3072]{2,1,0:T(8,128)(2,1)S(1)} collective-permute-done((bf16[4,24,3072]{2,1,0:T(8,128)(2,1)S(1)}, bf16[4,24,3072]{2,1,0:T(8,128)(2,1)S(1)}, u32[]{:S(2)}, u32[]{:S(2)}) %collective-permute-start.72) | collective-permute-done | bytes 589856 | tf_op jit(solution)/shard_map/ppermute | solution.py:48
  534.6 7.5 %collective-permute-done.59 = bf16[8,24,2304]{2,1,0:T(8,128)(2,1)S(1)} collective-permute-done((bf16[8,24,2304]{2,1,0:T(8,128)(2,1)S(1)}, bf16[8,24,2304]{2,1,0:T(8,128)(2,1)S(1)}, u32[]{:S(2)}, u32[]{:S(2)}) %collective-permute-start.59) | collective-permute-done | bytes 884768 | tf_op jit(solution)/shard_map/ppermute | solution.py:48
  (441 shorter events, 262.5 us)
Async XLA Ops:
  0.6 24.6 %collective-permute-start.10 = (bf16[1,24,2304]{2,1,0:T(8,128)(2,1)}, bf16[1,24,2304]{2,1,0:T(8,128)(2,1)S(1)}, u32[]{:S(2)}, u32[]{:S(2)}) collective-permute-start(bf16[1,24,2304]{2,1,0:T(8,128)(2,1)} %bitcast.269), channel_id=1, source_target_pairs={{0,8},{1,9},{2,10},{3,11},{4,12},{5,13},{6,14},{7,15},{8,0},{9,1},... | collective-permute-start | bytes 331784 | tf_op jit(solution)/shard_map/ppermute | solution.py:48
  3.7 21.5 %collective-permute-start.11 = (bf16[1,24,2304]{2,1,0:T(8,128)(2,1)}, bf16[1,24,2304]{2,1,0:T(8,128)(2,1)S(1)}, u32[]{:S(2)}, u32[]{:S(2)}) collective-permute-start(bf16[1,24,2304]{2,1,0:T(8,128)(2,1)} %bitcast.270), channel_id=1, source_target_pairs={{0,16},{1,17},{2,18},{3,19},{4,20},{5,21},{6,22},{7,23},{8,24},{9,... | collective-permute-start | bytes 331784 | tf_op jit(solution)/shard_map/ppermute | solution.py:48
  6.3 18.9 %collective-permute-start.12 = (bf16[1,24,2304]{2,1,0:T(8,128)(2,1)}, bf16[1,24,2304]{2,1,0:T(8,128)(2,1)S(1)}, u32[]{:S(2)}, u32[]{:S(2)}) collective-permute-start(bf16[1,24,2304]{2,1,0:T(8,128)(2,1)} %bitcast.271), channel_id=1, source_target_pairs={{0,24},{1,25},{2,26},{3,27},{4,28},{5,29},{6,30},{7,31},{8,16},{9,... | collective-permute-start | bytes 331784 | tf_op jit(solution)/shard_map/ppermute | solution.py:48
  39.8 24.7 %collective-permute-start.14 = (bf16[4,24,2304]{2,1,0:T(8,128)(2,1)S(1)}, bf16[4,24,2304]{2,1,0:T(8,128)(2,1)S(1)}, u32[]{:S(2)}, u32[]{:S(2)}) collective-permute-start(bf16[4,24,2304]{2,1,0:T(8,128)(2,1)S(1)} %pad_maximum_fusion.12.refs_0_), channel_id=1, source_target_pairs={{0,4},{1,5},{2,6},{3,7},{4,0},{5,1},{6,2},{7,3},{8,12},{9,13},{10,... | collective-permute-start | bytes 1327112 | tf_op jit(solution)/shard_map/ppermute | solution.py:48
  41.3 23.2 %collective-permute-start.15 = (bf16[4,24,2304]{2,1,0:T(8,128)(2,1)S(1)}, bf16[4,24,2304]{2,1,0:T(8,128)(2,1)S(1)}, u32[]{:S(2)}, u32[]{:S(2)}) collective-permute-start(bf16[4,24,2304]{2,1,0:T(8,128)(2,1)S(1)} %collective-permute-done.13.refs_1_), channel_id=1, source_target_pairs={{0,4},{1,5},{2,6},{3,7},{4,0},{5,1},{6,2},{7,3},{8,12},{9,13},{10,... | collective-permute-start | bytes 1327112 | tf_op jit(solution)/shard_map/ppermute | solution.py:48
  70.5 23.2 %collective-permute-start.34 = (bf16[4,24,3072]{2,1,0:T(8,128)(2,1)}, bf16[4,24,3072]{2,1,0:T(8,128)(2,1)}, u32[]{:S(2)}, u32[]{:S(2)}) collective-permute-start(bf16[4,24,3072]{2,1,0:T(8,128)(2,1)} %pad_maximum_fusion.10.refs_0_), channel_id=1, source_target_pairs={{0,4},{1,5},{2,6},{3,7},{4,0},{5,1},{6,2},{7,3},{8,12},{9,13},{10,... | collective-permute-start | bytes 1769480 | tf_op jit(solution)/shard_map/ppermute | solution.py:48
  71.0 25.0 %collective-permute-start.35 = (bf16[4,24,3072]{2,1,0:T(8,128)(2,1)}, bf16[4,24,3072]{2,1,0:T(8,128)(2,1)}, u32[]{:S(2)}, u32[]{:S(2)}) collective-permute-start(bf16[4,24,3072]{2,1,0:T(8,128)(2,1)} %pad_maximum_fusion.10.refs_0_), channel_id=1, source_target_pairs={{0,1},{1,0},{2,3},{3,2},{4,5},{5,4},{6,7},{7,6},{8,9},{9,8},{10,11... | collective-permute-start | bytes 1769480 | tf_op jit(solution)/shard_map/ppermute | solution.py:48
  93.6 26.3 %collective-permute-start.36 = (bf16[4,24,3072]{2,1,0:T(8,128)(2,1)}, bf16[4,24,3072]{2,1,0:T(8,128)(2,1)}, u32[]{:S(2)}, u32[]{:S(2)}) collective-permute-start(bf16[4,24,3072]{2,1,0:T(8,128)(2,1)} %collective-permute-done.34.refs_1_), channel_id=1, source_target_pairs={{0,1},{1,0},{2,3},{3,2},{4,5},{5,4},{6,7},{7,6},{8,9},{9,8},{10,11... | collective-permute-start | bytes 1769480 | tf_op jit(solution)/shard_map/ppermute | solution.py:48
  96.1 56.6 %collective-permute-start.20 = (bf16[2,512,768]{2,1,0:T(8,128)(2,1)}, bf16[2,512,768]{2,1,0:T(8,128)(2,1)}, u32[]{:S(2)}, u32[]{:S(2)}) collective-permute-start(bf16[2,512,768]{2,1,0:T(8,128)(2,1)} %pad_maximum_fusion.1), channel_id=1, source_target_pairs={{0,1},{2,3},{4,5},{6,7},{8,9},{10,11},{12,13},{14,15},{16,17},{18,... | collective-permute-start | bytes 4718600 | tf_op jit(solution)/shard_map/ppermute | solution.py:23
  100.6 20.8 %collective-permute-start.38 = (bf16[4,24,3072]{2,1,0:T(8,128)(2,1)}, bf16[4,24,3072]{2,1,0:T(8,128)(2,1)S(1)}, u32[]{:S(2)}, u32[]{:S(2)}) collective-permute-start(bf16[4,24,3072]{2,1,0:T(8,128)(2,1)} %collective-permute-done.34.refs_1_), channel_id=1, source_target_pairs={{0,2},{1,3},{2,0},{3,1},{4,6},{5,7},{6,4},{7,5},{8,10},{9,11},{10,... | collective-permute-start | bytes 1769480 | tf_op jit(solution)/shard_map/ppermute | solution.py:48
  224.3 95.3 %collective-permute-start.65 = (bf16[8,24,768]{2,1,0:T(8,128)(2,1)}, bf16[8,24,768]{2,1,0:T(8,128)(2,1)}, u32[]{:S(2)}, u32[]{:S(2)}) collective-permute-start(bf16[8,24,768]{2,1,0:T(8,128)(2,1)} %slice.540), channel_id=1, source_target_pairs={{0,4},{1,5},{2,6},{3,7},{4,0},{5,1},{6,2},{7,3},{8,12},{9,13},{10,... | collective-permute-start | bytes 884744 | tf_op jit(solution)/shard_map/ppermute | solution.py:48
  233.3 242.0 %collective-permute-start.76 = (bf16[16,96,768]{2,1,0:T(8,128)(2,1)}, bf16[16,96,768]{2,1,0:T(8,128)(2,1)}, u32[]{:S(2)}, u32[]{:S(2)}) collective-permute-start(bf16[16,96,768]{2,1,0:T(8,128)(2,1)} %get-tuple-element.226), channel_id=1, source_target_pairs={{0,2},{1,3},{2,0},{3,1},{4,6},{5,7},{6,4},{7,5},{8,10},{9,11},{10,... | collective-permute-start | bytes 7077896 | tf_op jit(solution)/shard_map/ppermute | solution.py:48
  318.3 126.4 %collective-permute-start.51 = (bf16[2,512,768]{1,2,0:T(8,128)(2,1)}, bf16[2,512,768]{1,2,0:T(8,128)(2,1)}, u32[]{:S(2)}, u32[]{:S(2)}) collective-permute-start(bf16[2,512,768]{1,2,0:T(8,128)(2,1)} %pad_maximum_fusion.4), channel_id=1, source_target_pairs={{1,0},{3,2},{5,4},{7,6},{9,8},{11,10},{13,12},{15,14},{17,16},{19,... | collective-permute-start | bytes 4718600 | tf_op jit(solution)/shard_map/ppermute | solution.py:23
  320.7 102.9 %collective-permute-start.66 = (bf16[4,24,768]{2,1,0:T(8,128)(2,1)S(1)}, bf16[4,24,768]{2,1,0:T(8,128)(2,1)S(1)}, u32[]{:S(2)}, u32[]{:S(2)}) collective-permute-start(bf16[4,24,768]{2,1,0:T(8,128)(2,1)S(1)} %slice.541), channel_id=1, source_target_pairs={{0,1},{1,0},{2,3},{3,2},{4,5},{5,4},{6,7},{7,6},{8,9},{9,8},{10,11... | collective-permute-start | bytes 442376 | tf_op jit(solution)/shard_map/ppermute | solution.py:48
  424.4 18.8 %collective-permute-start.67 = (bf16[1,24,768]{2,1,0:T(8,128)(2,1)S(1)}, bf16[1,24,768]{2,1,0:T(8,128)(2,1)S(1)}, u32[]{:S(2)}, u32[]{:S(2)}) collective-permute-start(bf16[1,24,768]{2,1,0:T(8,128)(2,1)S(1)} %get-tuple-element.355), channel_id=1, source_target_pairs={{0,8},{1,9},{2,10},{3,11},{4,12},{5,13},{6,14},{7,15},{8,0},{9,1},... | collective-permute-start | bytes 110600 | tf_op jit(solution)/shard_map/ppermute | solution.py:48
  443.1 34.8 %collective-permute-start.70 = (bf16[16,24,3072]{2,1,0:T(8,128)(2,1)}, bf16[16,24,3072]{2,1,0:T(8,128)(2,1)}, u32[]{:S(2)}, u32[]{:S(2)}) collective-permute-start(bf16[16,24,3072]{2,1,0:T(8,128)(2,1)} %get-tuple-element.224), channel_id=1, source_target_pairs={{0,2},{1,3},{2,0},{3,1},{4,6},{5,7},{6,4},{7,5},{8,10},{9,11},{10,... | collective-permute-start | bytes 7077896 | tf_op jit(solution)/shard_map/ppermute | solution.py:48
  470.9 20.6 %collective-permute-start.55 = (f32[1,1,256]{2,1,0:T(1,128)}, f32[1,1,256]{2,1,0:T(1,128)}, u32[]{:S(2)}, u32[]{:S(2)}) collective-permute-start(f32[1,1,256]{2,1,0:T(1,128)} %get-tuple-element.363), channel_id=1, source_target_pairs={{0,8},{1,9},{2,10},{3,11},{4,12},{5,13},{6,14},{7,15},{8,0},{9,1},... | collective-permute-start | bytes 3080 | tf_op jit(solution)/shard_map/ppermute | solution.py:48
  472.0 19.7 %collective-permute-start.56 = (f32[1,1,256]{2,1,0:T(1,128)}, f32[1,1,256]{2,1,0:T(1,128)}, u32[]{:S(2)}, u32[]{:S(2)}) collective-permute-start(f32[1,1,256]{2,1,0:T(1,128)} %get-tuple-element.365), channel_id=1, source_target_pairs={{0,16},{1,17},{2,18},{3,19},{4,20},{5,21},{6,22},{7,23},{8,24},{9,... | collective-permute-start | bytes 3080 | tf_op jit(solution)/shard_map/ppermute | solution.py:48
  477.8 24.9 %collective-permute-start.77 = (bf16[8,96,768]{2,1,0:T(8,128)(2,1)S(1)}, bf16[8,96,768]{2,1,0:T(8,128)(2,1)}, u32[]{:S(2)}, u32[]{:S(2)}) collective-permute-start(bf16[8,96,768]{2,1,0:T(8,128)(2,1)S(1)} %slice.531), channel_id=1, source_target_pairs={{0,1},{1,0},{2,3},{3,2},{4,5},{5,4},{6,7},{7,6},{8,9},{9,8},{10,11... | collective-permute-start | bytes 3538952 | tf_op jit(solution)/shard_map/ppermute | solution.py:48
  484.6 29.2 %collective-permute-start.71 = (bf16[8,24,3072]{2,1,0:T(8,128)(2,1)}, bf16[8,24,3072]{2,1,0:T(8,128)(2,1)}, u32[]{:S(2)}, u32[]{:S(2)}) collective-permute-start(bf16[8,24,3072]{2,1,0:T(8,128)(2,1)} %slice.532), channel_id=1, source_target_pairs={{0,4},{1,5},{2,6},{3,7},{4,0},{5,1},{6,2},{7,3},{8,12},{9,13},{10,... | collective-permute-start | bytes 3538952 | tf_op jit(solution)/shard_map/ppermute | solution.py:48
  491.6 25.2 %collective-permute-start.58 = (bf16[16,24,2304]{2,1,0:T(8,128)(2,1)}, bf16[16,24,2304]{2,1,0:T(8,128)(2,1)S(1)}, u32[]{:S(2)}, u32[]{:S(2)}) collective-permute-start(bf16[16,24,2304]{2,1,0:T(8,128)(2,1)} %get-tuple-element.220), channel_id=1, source_target_pairs={{0,2},{1,3},{2,0},{3,1},{4,6},{5,7},{6,4},{7,5},{8,10},{9,11},{10,... | collective-permute-start | bytes 5308424 | tf_op jit(solution)/shard_map/ppermute | solution.py:48
  517.2 24.9 %collective-permute-start.59 = (bf16[8,24,2304]{2,1,0:T(8,128)(2,1)S(1)}, bf16[8,24,2304]{2,1,0:T(8,128)(2,1)S(1)}, u32[]{:S(2)}, u32[]{:S(2)}) collective-permute-start(bf16[8,24,2304]{2,1,0:T(8,128)(2,1)S(1)} %slice.533), channel_id=1, source_target_pairs={{0,1},{1,0},{2,3},{3,2},{4,5},{5,4},{6,7},{7,6},{8,9},{9,8},{10,11... | collective-permute-start | bytes 2654216 | tf_op jit(solution)/shard_map/ppermute | solution.py:48
  522.4 34.4 %collective-permute-start.79 = (bf16[1,96,768]{2,1,0:T(8,128)(2,1)S(1)}, bf16[1,96,768]{2,1,0:T(8,128)(2,1)S(1)}, u32[]{:S(2)}, u32[]{:S(2)}) collective-permute-start(bf16[1,96,768]{2,1,0:T(8,128)(2,1)S(1)} %get-tuple-element.346), channel_id=1, source_target_pairs={{0,8},{1,9},{2,10},{3,11},{4,12},{5,13},{6,14},{7,15},{8,0},{9,1},... | collective-permute-start | bytes 442376 | tf_op jit(solution)/shard_map/ppermute | solution.py:48
  522.6 36.6 %collective-permute-start.80 = (bf16[1,96,768]{2,1,0:T(8,128)(2,1)S(1)}, bf16[1,96,768]{2,1,0:T(8,128)(2,1)S(1)}, u32[]{:S(2)}, u32[]{:S(2)}) collective-permute-start(bf16[1,96,768]{2,1,0:T(8,128)(2,1)S(1)} %get-tuple-element.348), channel_id=1, source_target_pairs={{0,16},{1,17},{2,18},{3,19},{4,20},{5,21},{6,22},{7,23},{8,24},{9,... | collective-permute-start | bytes 442376 | tf_op jit(solution)/shard_map/ppermute | solution.py:48
  (133 other events, 1986.6 us)
